TPU v7x, 512 devices: a whole 4x8x8 slice. The times are simulated.
512 devices in a mesh: rep: 16 (over z_lo, x), seq: 8 (over y), tp: 4 (over z_hi, core).
Axes of the slice: x: 4, y: 8, z: 8 (z_hi: 2, z_lo: 4; z = z_hi * 4 + z_lo), core: 2. Of those that a mesh axis runs over, the one named last changes fastest.
Arguments:
- prompt_q: bfloat16 [2, 8192, 4096], P(None, ('rep', 'seq'), 'tp'), may hold values from -130 to 130
- prompt_k: bfloat16 [2, 8192, 512], P(None, ('rep', 'seq'), 'tp'), may hold values from -10 to 10
- prompt_v: bfloat16 [2, 8192, 512], P(None, ('rep', 'seq'), 'tp'), may hold values from -24 to 24
- dec_q: bfloat16 [640, 4, 4096], P('rep', None, 'tp'), may hold values from -130 to 130
- dec_k: bfloat16 [640, 4, 512], P('rep', None, 'tp'), may hold values from -9 to 9
- dec_v: bfloat16 [640, 4, 512], P('rep', None, 'tp'), may hold values from -24 to 24
Outputs:
- prefill_out: bfloat16 [2, 8192, 4096], P(None, ('rep', 'seq'), 'tp')
- decode_out: bfloat16 [640, 4, 4096], P('rep', None, 'tp')
All inputs are finite; a program needn't handle non-finite values.
Results may differ from a plain program's by a relative error of at most 0.008.
Values may be sent and summed in bfloat16 or wider, within the bound.
A program may use at most 64 MiB of HBM per device.

v0:
```python
import math

import jax
import jax.numpy as jnp
from jax import lax
from jax.sharding import PartitionSpec as P

HEAD_WIDTH = 128


def joined(value, axis, join):
    pieces = jax.tree.map(lambda part: lax.all_gather(part, axis), value)
    head = jax.tree.map(lambda part: part[0], pieces)
    tail = jax.tree.map(lambda part: part[1:], pieces)
    running, _ = lax.scan(lambda running, piece: (join(running, piece), None), head, tail)
    return running


def absorb(state, scores, allowed, product_fn):
    top_old, weight_sum, weighted = state
    scores = jnp.where(allowed, scores, -jnp.inf)
    top_new = jnp.maximum(top_old, jnp.max(scores, axis=-1))
    anchor = jnp.where(jnp.isfinite(top_new), top_new, 0.0)
    shrink = jnp.exp(top_old - anchor)
    exponent = jnp.exp(scores - anchor[..., None])
    weight_sum = weight_sum * shrink + jnp.sum(exponent, axis=-1)
    weighted = weighted * shrink[..., None] + product_fn(exponent.astype(jnp.bfloat16))
    return (top_new, weight_sum, weighted)


def merge_partials(former, latter):
    top_new = jnp.maximum(former[0], latter[0])
    anchor = jnp.where(jnp.isfinite(top_new), top_new, 0.0)
    factor_one = jnp.exp(former[0] - anchor)
    factor_two = jnp.exp(latter[0] - anchor)
    weight_sum = former[1] * factor_one + latter[1] * factor_two
    weighted = former[2] * factor_one[..., None] + latter[2] * factor_two[..., None]
    return (top_new, weight_sum, weighted)


def fresh_state(kv_dev, group_size, row_count):
    return (
        jnp.full((kv_dev, group_size, row_count), -jnp.inf, jnp.float32),
        jnp.zeros((kv_dev, group_size, row_count), jnp.float32),
        jnp.zeros((kv_dev, group_size, row_count, HEAD_WIDTH), jnp.float32),
    )


def finalize_output(state):
    weighted = state[2] / state[1][..., None]
    kv_dev, group_size, row_count = state[1].shape
    return jnp.transpose(weighted, (2, 0, 1, 3)).reshape(
        row_count, kv_dev * group_size * HEAD_WIDTH
    )


def local(prompt_q, prompt_k, prompt_v, dec_q, dec_k, dec_v):
    row_count = prompt_q.shape[1]
    key_cols = prompt_k.shape[2]
    kv_dev = key_cols // HEAD_WIDTH
    group_size = prompt_q.shape[2] // key_cols
    score_scale = 1.0 / math.sqrt(HEAD_WIDTH)
    queries = prompt_q.reshape(2, row_count, kv_dev, group_size, HEAD_WIDTH)
    own_start = lax.axis_index(("rep", "seq")) * row_count
    query_index = own_start + jnp.arange(row_count)

    def fold_keys(states, key_block, value_block, key_first, key_width):
        key_index = key_first + jnp.arange(key_width)
        result = list(states)
        for query_half, key_half in ((0, 0), (1, 0), (1, 1)):
            single_keys = key_block[key_half].reshape(key_width, kv_dev, HEAD_WIDTH)
            single_values = value_block[key_half].reshape(key_width, kv_dev, HEAD_WIDTH)
            if query_half == 0:
                allowed = key_index[None, :] <= query_index[:, None]
                needed = key_first <= own_start + row_count - 1
            elif key_half == 0:
                allowed = True
                needed = None
            else:
                allowed = key_index[None, :] >= query_index[:, None]
                needed = key_first + key_width - 1 >= own_start

            def update(
                state,
                single_keys=single_keys,
                single_values=single_values,
                allowed=allowed,
                query_half=query_half,
            ):
                scores = (
                    jnp.einsum(
                        "yemi,fei->emyf",
                        queries[query_half],
                        single_keys,
                        preferred_element_type=jnp.float32,
                    )
                    * score_scale
                )

                def product_fn(attention_weights):
                    return jnp.einsum(
                        "vqha,avn->vqhn",
                        attention_weights,
                        single_values,
                        preferred_element_type=jnp.float32,
                    )

                return absorb(state, scores, allowed, product_fn)

            def unchanged(state):
                return state

            if needed is None:
                result[query_half] = update(result[query_half])
            else:
                result[query_half] = lax.cond(needed, update, unchanged, result[query_half])
        return tuple(result)

    initial = (
        fresh_state(kv_dev, group_size, row_count),
        fresh_state(kv_dev, group_size, row_count),
    )
    states = initial
    keys_piece = lax.all_gather(prompt_k, ("rep", "seq"), axis=1, tiled=True)
    values_piece = lax.all_gather(prompt_v, ("rep", "seq"), axis=1, tiled=True)
    piece_rows = keys_piece.shape[1]
    scan_block_size = math.gcd(piece_rows, 512)

    def advance(block_number, states):
        key_first = block_number * scan_block_size
        key_block = lax.dynamic_slice_in_dim(keys_piece, key_first, scan_block_size, 1)
        value_block = lax.dynamic_slice_in_dim(values_piece, key_first, scan_block_size, 1)
        return fold_keys(states, key_block, value_block, key_first, scan_block_size)

    states = lax.fori_loop(0, piece_rows // scan_block_size, advance, states)
    cache_k, cache_v = (
        lax.all_gather(prompt_k, "rep", axis=1, tiled=True),
        lax.all_gather(prompt_v, "rep", axis=1, tiled=True),
    )
    prefill_out = jnp.stack(
        [finalize_output(states[0]), finalize_output(states[1])], axis=0
    ).astype(jnp.bfloat16)
    sample_count = dec_q.shape[0]
    step_count = dec_q.shape[1]
    decode_row_block = dec_q.reshape(sample_count * step_count, kv_dev, group_size, HEAD_WIDTH)
    keys_all = cache_k.reshape(-1, kv_dev, HEAD_WIDTH)
    values_all = cache_v.reshape(-1, kv_dev, HEAD_WIDTH)
    total_keys = keys_all.shape[0]
    block_size = math.gcd(total_keys, 512)

    def prefix_advance(block_number, state):
        key_first = block_number * block_size
        single_keys = lax.dynamic_slice_in_dim(keys_all, key_first, block_size, 0)
        single_values = lax.dynamic_slice_in_dim(values_all, key_first, block_size, 0)
        scores = (
            jnp.einsum(
                "fvhl,ivl->vhfi", decode_row_block, single_keys, preferred_element_type=jnp.float32
            )
            * score_scale
        )

        def product_fn(attention_weights):
            return jnp.einsum(
                "yiop,pyx->yiox",
                attention_weights,
                single_values,
                preferred_element_type=jnp.float32,
            )

        return absorb(state, scores, True, product_fn)

    prefix_state = lax.fori_loop(
        0,
        total_keys // block_size,
        prefix_advance,
        fresh_state(kv_dev, group_size, sample_count * step_count),
    )
    merged = joined(prefix_state, "seq", merge_partials)
    suffix_q = dec_q.reshape(sample_count, step_count, kv_dev, group_size, HEAD_WIDTH)
    suffix_k = dec_k.reshape(sample_count, step_count, kv_dev, HEAD_WIDTH)
    suffix_v = dec_v.reshape(sample_count, step_count, kv_dev, HEAD_WIDTH)
    suffix_scores = (
        jnp.einsum("njkgd,nukd->kgnju", suffix_q, suffix_k, preferred_element_type=jnp.float32)
        * score_scale
    )
    suffix_scores = suffix_scores.reshape(kv_dev, group_size, sample_count * step_count, step_count)
    step_index = jnp.arange(sample_count * step_count) % step_count
    allowed = jnp.arange(step_count)[None, :] <= step_index[:, None]

    def suffix_product(attention_weights):
        shaped = attention_weights.reshape(kv_dev, group_size, sample_count, step_count, step_count)
        mixed = jnp.einsum(
            "kgnju,nukd->kgnjd", shaped, suffix_v, preferred_element_type=jnp.float32
        )
        return mixed.reshape(kv_dev, group_size, sample_count * step_count, HEAD_WIDTH)

    closing_state = absorb(merged, suffix_scores, allowed, suffix_product)
    decode_flat = closing_state[2] / closing_state[1][..., None]
    decode_flat = decode_flat.reshape(kv_dev, group_size, sample_count, step_count, HEAD_WIDTH)
    decode_out = jnp.transpose(decode_flat, (2, 3, 0, 1, 4)).reshape(
        sample_count, step_count, kv_dev * group_size * HEAD_WIDTH
    )
    return (prefill_out, decode_out.astype(jnp.bfloat16))


def solution(mesh):
    placed = (
        P(None, ("rep", "seq"), "tp"),
        P(None, ("rep", "seq"), "tp"),
        P(None, ("rep", "seq"), "tp"),
        P("rep", None, "tp"),
        P("rep", None, "tp"),
        P("rep", None, "tp"),
    )
    return jax.shard_map(
        local,
        mesh=mesh,
        in_specs=placed,
        out_specs=(P(None, ("rep", "seq"), "tp"), P("rep", None, "tp")),
        check_vma=False,
    )
```

profile of v0, /device:TPU:8, one launch (start us, length us, event | category | flops | bytes accessed | tf_op | source)
XLA Modules:
  0.0 1498.7 jit_solution(6102513773404683181)
XLA Ops:
  8.7 1.1 reshape.334
  10.6 50.4 %all_gather.32 = bf16[2,1024,128]{2,1,0:T(8,128)(2,1)} all-gather(bf16[2,64,128]{2,1,0:T(8,128)(2,1)} %param.17), channel_id=1, replica_groups=mesh['rep'=16,'seq'=8,'tp'=4] {'rep'}, dimensions={1}, use_global_device_ids=true | all-gather | bytes 557056 | tf_op jit(solution)/shard_map/all_gather | solution.py:137
  61.1 42.2 %all_gather.33 = bf16[2,1024,128]{2,1,0:T(8,128)(2,1)} all-gather(bf16[2,64,128]{2,1,0:T(8,128)(2,1)} %param.18), channel_id=1, replica_groups=mesh['rep'=16,'seq'=8,'tp'=4] {'rep'}, dimensions={1}, use_global_device_ids=true | all-gather | bytes 557056 | tf_op jit(solution)/shard_map/all_gather | solution.py:138
  103.3 17.5 %while.63 = (s32[]{:T(128)}, f32[1,8,160]{2,1,0:T(8,128)S(1)}, f32[1,8,160]{2,1,0:T(8,128)S(1)}, f32[1,8,160,128]{3,2,1,0:T(8,128)S(1)}, bf16[2048,1,128]{2,0,1:...) while((s32[]{:T(128)}, f32[1,8,160]{2,1,0:T(8,128)S(1)}, ...), condition=%wide.region_15.16_spmd.clone, body=%wide.region_12.15_spmd.clone.sunk | while | flops 341294080 | bytes 9857207 | solution.py:172
  103.3 1.7 bitcast_reduce_fusion.2
  105.9 1.7 fusion.122
  107.7 1.7 bitcast_reduce_fusion.2
  110.3 1.7 fusion.122
  112.1 1.7 bitcast_reduce_fusion.2
  114.7 1.7 fusion.122
  116.5 1.7 bitcast_reduce_fusion.2
  119.1 1.7 fusion.122
  121.7 1.1 reshape.336
  122.8 25.5 %all-gather = f32[8,8,160]{2,1,0:T(8,128)S(1)} all-gather(f32[1,8,160]{2,1,0:T(8,128)S(1)} %get-tuple-element.723), channel_id=2, replica_groups=mesh['rep'=16,'seq'=8,'tp'=4] {'seq'}, dimensions={0}, use_global_device_ids=true | all-gather | bytes 46080 | tf_op jit(solution)/shard_map/all_gather | solution.py:12
  148.4 24.6 %all-gather.1 = f32[8,8,160]{2,1,0:T(8,128)S(1)} all-gather(f32[1,8,160]{2,1,0:T(8,128)S(1)} %get-tuple-element.724), channel_id=3, replica_groups=mesh['rep'=16,'seq'=8,'tp'=4] {'seq'}, dimensions={0}, use_global_device_ids=true | all-gather | bytes 46080 | tf_op jit(solution)/shard_map/all_gather | solution.py:12
  174.2 1.6 fusion.96
  175.8 530.4 %all-gather.7.cloned.1.call-done = bf16[2,8192,128]{2,1,0:T(8,128)(2,1)} async-done(((bf16[2,64,128]{2,1,0:T(8,128)(2,1)}), bf16[2,8192,128]{2,1,0:T(8,128)(2,1)}) %all-gather.7.cloned.1.call-update) | async-done | bytes 4194320 | tf_op jit(solution)/shard_map/all_gather | solution.py:124
  706.1 689.0 %all-gather.9.cloned.1.call-done = bf16[2,8192,128]{2,1,0:T(8,128)(2,1)} async-done(((bf16[2,64,128]{2,1,0:T(8,128)(2,1)}), bf16[2,8192,128]{2,1,0:T(8,128)(2,1)}) %all-gather.9.cloned.1.call-update) | async-done | bytes 4194320 | tf_op jit(solution)/shard_map/all_gather | solution.py:125
  1395.2 76.0 %while.64 = (s32[]{:T(128)}, f32[1,8,64]{2,1,0:T(8,128)S(1)}, f32[1,8,64]{2,1,0:T(8,128)S(1)}, f32[1,8,64,128]{3,2,1,0:T(8,128)S(1)}, f32[1,8,64]{2,1,0:T(8,128)...) while((s32[]{:T(128)}, f32[1,8,64]{2,1,0:T(8,128)S(1)}, ...), condition=%wide.region_11.12_spmd.clone.clone, body=%wide.region_0.11_spmd.clone.clone.sunk | while | flops 408369216 | bytes 14799867 | solution.py:135
  1396.3 1.2 conditional.8
  1399.8 1.2 conditional.9
  1404.5 1.2 conditional.9
  1409.2 1.2 conditional.9
  1413.8 1.2 conditional.9
  1418.5 1.2 conditional.9
  1422.1 1.1 constant_dynamic-slice_fusion.7
  1423.2 1.2 conditional.9
  1427.9 1.2 conditional.9
  1432.6 1.2 conditional.9
  1436.2 1.1 constant_dynamic-slice_fusion.7
  1437.2 1.2 conditional.9
  1441.9 1.2 conditional.9
  1446.6 1.2 conditional.9
  1450.2 1.1 constant_dynamic-slice_fusion.7
  1451.3 1.2 conditional.9
  1455.9 1.2 conditional.9
  1460.6 1.2 conditional.9
  1465.3 1.2 conditional.9
  1469.9 1.2 conditional.9
  1472.5 5.0 slice_bitcast_fusion
  1477.4 12.3 while.62
  1477.5 1.7 fusion.116
  1479.3 1.7 fusion.116
  1481.0 1.7 fusion.116
  1482.8 1.7 fusion.116
  1484.5 1.7 fusion.116
  1486.3 1.7 fusion.116
  1488.0 1.7 fusion.116
  (453 shorter events, 81.7 us)
Async XLA Ops:
  7.2 1483.0 %copy-start = (bf16[40,4,128]{2,1,0:T(4,128)(2,1)S(1)}, bf16[40,4,128]{2,1,0:T(4,128)(2,1)}, u32[]{:S(2)}) copy-start(bf16[40,4,128]{2,1,0:T(4,128)(2,1)} %param.21) | copy-start | bytes 122884
  7.2 698.9 %all-gather.7.cloned.1.call-start = ((), (), s32[]{:S(2)}) async-start(), calls=%async_computation | async-start | bytes 4227072 | tf_op jit(solution)/shard_map/all_gather | solution.py:124
  7.9 1387.2 %all-gather.9.cloned.1.call-start = ((), (), s32[]{:S(2)}) async-start(), calls=%async_computation.1 | async-start | bytes 4227072 | tf_op jit(solution)/shard_map/all_gather | solution.py:125
  8.7 1463.8 %all-gather.11.cloned.1.call-start = ((), (), s32[]{:S(2)}) async-start(), calls=%async_computation.2 | async-start | bytes 5898240 | tf_op jit(solution)/shard_map/all_gather | solution.py:12
  120.8 0.8 copy-start.1
  120.8 53.4 %copy-start.4 = (bf16[40,4,128]{2,1,0:T(4,128)(2,1)S(1)}, bf16[40,4,128]{2,1,0:T(4,128)(2,1)}, u32[]{:S(2)}) copy-start(bf16[40,4,128]{2,1,0:T(4,128)(2,1)} %param.20) | copy-start | bytes 122884
  148.4 1246.8 %copy-start.2 = (f32[8,8,160]{2,1,0:T(8,128)}, f32[8,8,160]{2,1,0:T(8,128)S(1)}, u32[]{:S(2)}) copy-start(f32[8,8,160]{2,1,0:T(8,128)S(1)} %all-gather) | copy-start | bytes 122884
  173.0 1222.2 %copy-start.3 = (f32[8,8,160]{2,1,0:T(8,128)}, f32[8,8,160]{2,1,0:T(8,128)S(1)}, u32[]{:S(2)}) copy-start(f32[8,8,160]{2,1,0:T(8,128)S(1)} %all-gather.1) | copy-start | bytes 122884
  1472.5 5.0 slice-start
  1472.5 5.0 slice-start.1
  1472.5 5.0 slice-start.2
Sparse Core Ops, SparseCore 0:
  10.1 695.9 all-gather.6
  708.2 686.8 all-gather.8
  1397.2 61.4 all-gather.10
where the time goes:
time: 1500 us
  waiting for transfers between devices  1220 us (81%)
  blocking collectives  143 us (10%)
  local copies, waits for them, and re-layouts  46.1 us (3%)
  matrix products  40.6 us (3%)
  other arithmetic  30.6 us (2%)
    all_gather x1, waiting for transfers between devices, local(): values_piece = lax.all_gather(prompt_v, ('rep', 'seq'), axis=1, tiled=True)  689 us
    all_gather x1, waiting for transfers between devices, local(): keys_piece = lax.all_gather(prompt_k, ('rep', 'seq'), axis=1, tiled=True)  530 us
    all_gather x1, blocking collectives, local(): lax.all_gather(prompt_k, 'rep', axis=1, tiled=True)  50.4 us
    all_gather x2, blocking collectives, joined(): pieces = jax.tree.map(lambda part: lax.all_gather(part, axis), value)  50.1 us
    all_gather x1, blocking collectives, local(): lax.all_gather(prompt_v, 'rep', axis=1, tiled=True)  42.2 us
  transfers between devices with their start and end apart: 3, of which 2 were waited for; matrix products, arithmetic and copies ran while one was open for 6% of the time, Pallas kernels for 0%

commit v1 on v0

v1 whole, which is shorter than its diff:
```python
import math

import jax
import jax.numpy as jnp
from jax import lax
from jax.experimental import pallas as pl
from jax.experimental.pallas import tpu as pltpu
from jax.sharding import PartitionSpec as P

WIDTH = 128
MESH = pl.DeviceIdType.MESH
SCALE = math.log2(math.e) / math.sqrt(WIDTH)
LOW = -1e30
NT = (((1,), (1,)), ((), ()))
NX, NY, NZ = 4, 8, 4
TOK = 64
GROUP = 8
HALF = TOK * GROUP
MAIN = 2 * HALF
DEC = 160
ROWS = MAIN + DEC
KEYS = NY * TOK
CUT = ROWS // 2
BLOCK = 128
F32, BF16 = jnp.float32, jnp.bfloat16


def kernel(
    pq, pk, pv, dqkv, out, dout,
    qbuf, kv, acc, top, part, stat, got, gstat, mid, mstat, dgat,
    zs, zr, ys, yr, qs, qr, ms, mr, fs, fr, ds, dr,
):
    rep, y, tp = lax.axis_index("rep"), lax.axis_index("seq"), lax.axis_index("tp")
    z, x = rep // NX, rep % NX

    def at(zz, xx, yy):
        return (zz * NX + xx, yy, tp)

    right, left = at(z, (x + 1) % NX, y), at(z, (x + NX - 1) % NX, y)
    ynext, yprev = at(z, x, (y + 1) % NY), at(z, x, (y + NY - 1) % NY)
    stacked = [at((z + j) % NZ, x, y) for j in range(1, NZ)]
    peers = (right, left, ynext, yprev, *stacked)

    def send(src, dst, ssem, rsem, dev):
        return pltpu.make_async_remote_copy(
            src_ref=src, dst_ref=dst, send_sem=ssem, recv_sem=rsem, device_id=dev, device_id_type=MESH
        )

    barrier = pltpu.get_barrier_semaphore()
    for dev in peers:
        pl.semaphore_signal(barrier, inc=1, device_id=dev, device_id_type=MESH)

    kv[z, :, 0:TOK, 0:WIDTH] = pk[...]
    kv[z, :, 0:TOK, WIDTH : 2 * WIDTH] = pv[...]
    for half in range(2):
        for g in range(GROUP):
            qbuf[0, half * HALF + g * TOK : half * HALF + (g + 1) * TOK, :] = pq[
                half, :, g * WIDTH : (g + 1) * WIDTH
            ]
    qbuf[0, MAIN:ROWS, :] = dqkv[0]

    pl.semaphore_wait(barrier, len(peers))

    planes = (
        z,
        jnp.where(z == 0, 1, z - 1),
        jnp.where(z < 2, 2, jnp.where(z == 2, 3, 1)),
        jnp.where(z < 2, 3, 0),
    )

    def plane_at(k):
        return jnp.where(k == 0, planes[0], jnp.where(k == 1, planes[1], jnp.where(k == 2, planes[2], planes[3])))

    def slot(p, r):
        return kv.at[p, :, pl.ds(r * TOK, TOK), :]

    def slot_half(p, r, half):
        return kv.at[p, half, pl.ds(r * TOK, TOK), :]

    def z_copy(j):
        own = slot(z, 0)
        return send(own, own, zs.at[j - 1], zr.at[z], stacked[j - 1])

    def z_arrive(p):
        here = slot(p, 0)
        send(here, here, zs.at[0], zr.at[p], right).wait_recv()

    def y_copies(p, d):
        if d == 1:
            a, b = slot(p, 0), slot(p, 0)
        else:
            a, b = slot(p, 2 * d - 3), slot(p, 2 * d - 2)
        if d < 4:
            return (
                send(a, slot(p, 2 * d - 1), ys.at[p, 2 * d - 2], yr.at[p, 2 * d - 2], ynext),
                send(b, slot(p, 2 * d), ys.at[p, 2 * d - 1], yr.at[p, 2 * d - 1], yprev),
            )
        return (
            send(slot_half(p, 5, 0), slot_half(p, 7, 0), ys.at[p, 6], yr.at[p, 6], ynext),
            send(slot_half(p, 6, 1), slot_half(p, 7, 1), ys.at[p, 7], yr.at[p, 7], yprev),
        )

    def z_step(k):
        if k == 0:
            for j in range(1, NZ):
                z_copy(j).start()
        else:
            z_arrive(planes[k])
        for copy in y_copies(planes[k], 1):
            copy.start()

    def y_step(k, d):
        p = planes[k]
        for copy in y_copies(p, d):
            copy.wait_recv()
        if d < 4:
            for copy in y_copies(p, d + 1):
                copy.start()

    first, second = pl.ds(0, CUT), pl.ds(CUT, CUT)

    def q_copy(i):
        src, dst, rows, dev = (
            (0, 1, first, right),
            (0, 3, second, left),
            (0, 1, second, right),
            (0, 3, first, left),
            (1, 2, first, right),
            (3, 2, second, left),
        )[i]
        return send(qbuf.at[src, rows, :], qbuf.at[dst, rows, :], qs.at[i], qr.at[i], dev)

    def q_forward():
        q_copy(0).wait_recv()
        q_copy(4).start()
        q_copy(1).wait_recv()
        q_copy(5).start()

    def values(p, half):
        v = kv[p, half, :, WIDTH : 2 * WIDTH]
        return kv[p, half, :, 0:WIDTH], jnp.concatenate([v, jnp.ones_like(v)], axis=1)

    def update(s, r0, n, keys, vals, allowed=None):
        rows = pl.ds(r0, n)
        scores = lax.dot_general(qbuf[s, rows, :], keys, NT, preferred_element_type=F32)
        if allowed is not None:
            scores = jnp.where(allowed, scores, LOW)
        top_old = top[s, rows, :]
        top_new = jnp.maximum(top_old, jnp.max(scores, axis=-1, keepdims=True) * SCALE)
        shrink = jnp.exp2(top_old - top_new)
        span = scores.shape[1]
        anchor = top_new[:, 0:1] if span % WIDTH else jnp.tile(top_new, (1, span // WIDTH))
        weights = jnp.exp2(scores * SCALE - anchor).astype(BF16)
        top[s, rows, :] = top_new
        acc[s, rows, :] = acc[s, rows, :] * jnp.concatenate([shrink, shrink], axis=1) + jnp.dot(
            weights, vals, preferred_element_type=F32
        )

    def main_rows(s, p, h, lo, hi):
        k0, v0 = values(p, 0)
        for j in range(lo, hi):
            update(s, HALF + j * BLOCK, BLOCK, k0, v0)
        kh, vh = values(p, h)
        for j in range(lo, hi):
            update(s, pl.multiple_of(h * HALF + j * BLOCK, BLOCK), BLOCK, kh, vh)

    def dec_rows(s, p):
        for half in range(2):
            kk, vv = values(p, half)
            update(s, MAIN, DEC, kk, vv)

    def which(s, k, p):
        far = (x + jnp.where(s == 1, 3, jnp.where(s == 3, 1, 2))) % NX
        return jnp.where(k == 0, jnp.where(x < far, 0, 1), jnp.where(p < z, 0, 1))

    def eye(n):
        return lax.broadcasted_iota(jnp.int32, (n, WIDTH), 0) == lax.broadcasted_iota(jnp.int32, (n, WIDTH), 1)

    def finish(s, r0, n, target, starget, row, count):
        rows = pl.ds(r0, n)
        total = acc[s, rows, WIDTH : 2 * WIDTH]
        target[rows, :] = (acc[s, rows, 0:WIDTH] / jnp.maximum(total, 1e-30)).astype(BF16)
        mask = eye(n)
        starget[row : row + 1, :] = jnp.sum(jnp.where(mask, top[s, rows, :], 0.0), axis=0, keepdims=True)
        starget[row + count : row + count + 1, :] = jnp.sum(jnp.where(mask, total, 0.0), axis=0, keepdims=True)

    def merge(s, r0, n, source, ssource, row, count):
        rows = pl.ds(r0, n)
        mask = eye(n)

        def column(r):
            return jnp.sum(jnp.where(mask, ssource[r : r + 1, :], 0.0), axis=1, keepdims=True)

        top_in, sum_in = column(row), column(row + count)
        top_old = top[s, rows, :]
        top_new = jnp.maximum(top_old, top_in)
        shrink = jnp.exp2(top_old - top_new)
        gain = jnp.exp2(top_in - top_new) * sum_in
        top[s, rows, :] = top_new
        acc[s, rows, 0:WIDTH] = acc[s, rows, 0:WIDTH] * shrink + source[rows, :].astype(F32) * gain
        acc[s, rows, WIDTH : 2 * WIDTH] = acc[s, rows, WIDTH : 2 * WIDTH] * shrink + gain

    def section(c):
        if c < 2:
            return [(c * HALF + j * BLOCK, BLOCK, j) for j in range(4)], 4, c * HALF, HALF
        first_row = MAIN + (c - 2) * (DEC // 2)
        return [(first_row, DEC // 2, 0)], 1, first_row, DEC // 2

    def finish_section(s, c):
        blocks, count, _, _ = section(c)
        for r0, n, j in blocks:
            finish(s, r0, n, part.at[s], stat.at[s, c], j, count)

    def merge_section(s, c, source, ssource):
        blocks, count, _, _ = section(c)
        for r0, n, j in blocks:
            merge(s, r0, n, source, ssource.at[c], j, count)

    def relay_copies(c):
        _, _, r0, n = section(c)
        rows, dev = pl.ds(r0, n), (right, left)[c % 2]
        return (
            send(part.at[2, rows, :], mid.at[rows, :], ms.at[c], mr.at[c], dev),
            send(stat.at[2, c], mstat.at[c], ms.at[4 + c], mr.at[4 + c], dev),
        )

    def final_copies(s, c):
        _, _, r0, n = section(c)
        rows, side = pl.ds(r0, n), 0 if s == 1 else 1
        dev, i = (left, right)[side], 4 * side + c
        return (
            send(part.at[s, rows, :], got.at[side, rows, :], fs.at[i], fr.at[i], dev),
            send(stat.at[s, c], gstat.at[side, c], fs.at[8 + i], fr.at[8 + i], dev),
        )

    def start(copies):
        for copy in copies:
            copy.start()

    def arrive(copies):
        for copy in copies:
            copy.wait_recv()

    def take_relay(c):
        arrive(relay_copies(c))
        merge_section((3, 1)[c % 2], c, mid, mstat)

    def take_final(c):
        for s in (1, 3):
            arrive(final_copies(s, c))
        for side in range(2):
            merge_section(0, c, got.at[side], gstat.at[side])

    def d_copies(d):
        if d == 1:
            a, b = 0, 0
        else:
            a, b = 2 * d - 3, 2 * d - 2
        if d < 4:
            return (
                send(dgat.at[a], dgat.at[2 * d - 1], ds.at[2 * d - 2], dr.at[2 * d - 2], ynext),
                send(dgat.at[b], dgat.at[2 * d], ds.at[2 * d - 1], dr.at[2 * d - 1], yprev),
            )
        top_rows, low_rows = pl.ds(0, DEC // 2), pl.ds(DEC // 2, DEC // 2)
        return (
            send(dgat.at[5, top_rows, :], dgat.at[7, top_rows, :], ds.at[6], dr.at[6], ynext),
            send(dgat.at[6, low_rows, :], dgat.at[7, low_rows, :], ds.at[7], dr.at[7], yprev),
        )

    def place(r):
        delta = -(r + 1) // 2 if r % 2 else r // 2
        column = pl.multiple_of(((y + delta + NY) % NY) * WIDTH, WIDTH)
        dout[:, pl.ds(column, WIDTH)] = dgat[r]

    def d_step(d):
        arrive(d_copies(d))
        if d < 4:
            start(d_copies(d + 1))
            place(2 * d - 1)
            place(2 * d)
        else:
            place(7)

    z_step(0)
    for i in range(4):
        q_copy(i).start()

    for s in range(4):
        acc[s] = jnp.zeros((ROWS, 2 * WIDTH), F32)
        top[s] = jnp.full((ROWS, WIDTH), LOW, F32)

    step_row = lax.broadcasted_iota(jnp.int32, (DEC, DEC), 0)
    step_col = lax.broadcasted_iota(jnp.int32, (DEC, DEC), 1)
    own_v = dqkv[2]
    update(
        0, MAIN, DEC, dqkv[1], jnp.concatenate([own_v, jnp.ones_like(own_v)], axis=1),
        (step_row // 4 == step_col // 4) & (step_col <= step_row),
    )

    y_step(0, 1)
    z_step(1)
    y_step(0, 2)
    y_step(1, 1)
    z_step(2)
    q_forward()
    y_step(0, 3)
    y_step(1, 2)
    y_step(0, 4)

    p0 = planes[0]
    key_col = lax.broadcasted_iota(jnp.int32, (BLOCK, KEYS), 1)
    key_slot = key_col // TOK
    key_delta = jnp.where(key_slot % 2 == 1, NY - (key_slot + 1) // 2, key_slot // 2)
    key_index = ((y + key_delta) % NY) * TOK + key_col % TOK
    query_index = y * TOK + lax.broadcasted_iota(jnp.int32, (BLOCK, KEYS), 0) % TOK
    for half in range(2):
        kk, vv = values(p0, half)
        allowed = key_index <= query_index if half == 0 else key_index >= query_index
        for j in range(4):
            update(0, half * HALF + j * BLOCK, BLOCK, kk, vv, allowed)
    y_step(1, 3)
    k0, v0 = values(p0, 0)
    for j in range(4):
        update(0, HALF + j * BLOCK, BLOCK, k0, v0)
    dec_rows(0, p0)
    y_step(2, 1)

    unit_rows = (0, 1, 3, 2, 0, 1, 3, 2, 2, 1, 2, 1, 3, 3, 0, 0)
    unit_plane = (0, 0, 0, 0, 1, 1, 1, 1, 2, 2, 3, 3, 2, 3, 2, 3)

    def lookup(table, t):
        value = jnp.int32(table[0])
        for i in range(1, len(table)):
            value = jnp.where(t == i, table[i], value)
        return value

    def send_finished(s, *sections):
        for c in sections:
            finish_section(s, c)
            start(relay_copies(c) if s == 2 else final_copies(s, c))

    def sampled_last():
        def one(i, carry):
            dec_rows(i // 2, plane_at(2 + i % 2))
            return carry

        lax.fori_loop(0, 8, one, 0)
        send_finished(2, 2, 3)

    def sampled_relay():
        take_relay(2)
        take_relay(3)
        send_finished(1, 2, 3)
        send_finished(3, 2, 3)

    def sampled_out():
        take_final(2)
        take_final(3)
        rows = pl.ds(MAIN, DEC)
        dgat[0] = (acc[0, rows, 0:WIDTH] / acc[0, rows, WIDTH : 2 * WIDTH]).astype(BF16)
        start(d_copies(1))
        place(0)

    def left_relay():
        take_relay(1)
        send_finished(1, 1)

    def right_done():
        send_finished(3, 1)
        take_relay(0)
        send_finished(3, 0)
        d_step(1)

    middle = {
        1: lambda: y_step(1, 4),
        2: lambda: y_step(2, 2),
        3: lambda: y_step(2, 3),
        4: lambda: y_step(3, 2),
        5: lambda: y_step(2, 4),
        6: lambda: y_step(3, 3),
        8: lambda: y_step(3, 4),
        11: sampled_relay,
        12: left_relay,
        14: lambda: d_step(2),
        15: lambda: d_step(4),
    }
    after = {
        1: lambda: z_step(3),
        2: lambda: y_step(3, 1),
        9: sampled_last,
        10: lambda: send_finished(2, 0, 1),
        11: lambda: send_finished(1, 0),
        12: sampled_out,
        13: right_done,
        14: lambda: d_step(3),
    }
    before = {
        1: lambda: q_copy(2).wait_recv(),
        2: lambda: q_copy(3).wait_recv(),
        3: lambda: (q_copy(4).wait_recv(), q_copy(5).wait_recv())[0],
    }

    def hook(table, t):
        for i, step in table.items():
            pl.when(t == i)(step)

    def unit(t, carry):
        hook(before, t)
        k, s = lookup(unit_plane, t), lookup(unit_rows, t)
        p = plane_at(k)
        h = which(s, k, p)
        main_rows(s, p, h, 0, 2)
        hook(middle, t)
        main_rows(s, p, h, 2, 4)
        pl.when(t < 8)(lambda: dec_rows(s, p))
        hook(after, t)
        return carry

    lax.fori_loop(1, 16, unit, 0)
    for c in (0, 1):
        take_final(c)
        for g in range(GROUP):
            rows = pl.ds(c * HALF + g * TOK, TOK)
            out[c, :, g * WIDTH : (g + 1) * WIDTH] = (
                acc[0, rows, 0:WIDTH] / acc[0, rows, WIDTH : 2 * WIDTH]
            ).astype(BF16)

    for j in range(1, NZ):
        z_copy(j).wait_send()
    for p in range(NZ):
        for d in range(1, 5):
            for copy in y_copies(p, d):
                copy.wait_send()
    for i in range(6):
        q_copy(i).wait_send()
    for c in range(4):
        for copy in (*relay_copies(c), *final_copies(1, c), *final_copies(3, c), *d_copies(c + 1)):
            copy.wait_send()


def local(prompt_q, prompt_k, prompt_v, dec_q, dec_k, dec_v):
    head = lax.axis_index("seq") * WIDTH
    mine = lax.dynamic_slice_in_dim(dec_q, head, WIDTH, 2)
    dqkv = jnp.stack([mine, dec_k, dec_v]).reshape(3, DEC, WIDTH)
    vmem = pl.BlockSpec(memory_space=pltpu.VMEM)
    dma = pltpu.SemaphoreType.DMA
    prefill_out, decode_out = pl.pallas_call(
        kernel,
        out_shape=(
            jax.ShapeDtypeStruct((2, TOK, GROUP * WIDTH), BF16),
            jax.ShapeDtypeStruct((DEC, GROUP * WIDTH), BF16),
        ),
        in_specs=[vmem] * 4,
        out_specs=(vmem, vmem),
        scratch_shapes=[
            pltpu.VMEM((4, ROWS, WIDTH), BF16),
            pltpu.VMEM((NZ, 2, KEYS, 2 * WIDTH), BF16),
            pltpu.VMEM((4, ROWS, 2 * WIDTH), F32),
            pltpu.VMEM((4, ROWS, WIDTH), F32),
            pltpu.VMEM((4, ROWS, WIDTH), BF16),
            pltpu.VMEM((4, 4, 8, WIDTH), F32),
            pltpu.VMEM((2, ROWS, WIDTH), BF16),
            pltpu.VMEM((2, 4, 8, WIDTH), F32),
            pltpu.VMEM((ROWS, WIDTH), BF16),
            pltpu.VMEM((4, 8, WIDTH), F32),
            pltpu.VMEM((8, DEC, WIDTH), BF16),
            dma((NZ,)),
            dma((NZ,)),
            dma((NZ, 8)),
            dma((NZ, 8)),
            dma((6,)),
            dma((6,)),
            dma((8,)),
            dma((8,)),
            dma((16,)),
            dma((16,)),
            dma((8,)),
            dma((8,)),
        ],
        compiler_params=pltpu.CompilerParams(
            collective_id=0, has_side_effects=True, vmem_limit_bytes=48 << 20
        ),
    )(prompt_q, prompt_k, prompt_v, dqkv)
    return prefill_out, decode_out.reshape(dec_q.shape)


def solution(mesh):
    placed = (
        P(None, ("rep", "seq"), "tp"),
        P(None, ("rep", "seq"), "tp"),
        P(None, ("rep", "seq"), "tp"),
        P("rep", None, "tp"),
        P("rep", None, "tp"),
        P("rep", None, "tp"),
    )
    return jax.shard_map(
        local,
        mesh=mesh,
        in_specs=placed,
        out_specs=(P(None, ("rep", "seq"), "tp"), P("rep", None, "tp")),
        check_vma=False,
    )
```

time: 1500 us -> 84.4 us (0.06)
  waiting for transfers between devices: 1220 us -> 0 us
  blocking collectives: 143 us -> 0 us
  Pallas kernels: 0 us -> 80.1 us
  local copies, waits for them, and re-layouts: 46.1 us -> 2.54 us
  matrix products: 40.6 us -> 0 us
  other arithmetic: 30.6 us -> 0.82 us
    all_gather x3 -> x0, waiting for transfers between devices: 1220 us -> none  [the longest x1 689 us: local(): values_piece = lax.all_gather(prompt_v, ('rep', 'seq'), axis=1, tiled=True)]
    all_gather x4 -> x0, blocking collectives: 143 us -> none  [the longest x1 50.4 us: local(): lax.all_gather(prompt_k, 'rep', axis=1, tiled=True)]
    pallas_call x0 -> x1, Pallas kernels: none -> 80.1 us  [local(): pl.pallas_call(kernel, out_shape=(jax.ShapeDtypeStruct((2, TOK, GROUP * W...]
    dot_general x76 -> x0, matrix products: 40.6 us -> none  [the longest x33 12.8 us: product_fn(): jnp.einsum('vqha,avn->vqhn', attention_weights, single_values, preferred_...]
    dynamic_slice x16 -> x1, local copies, waits for them, and re-layouts: 17.3 us -> 0.02 us  [local(): mine = lax.dynamic_slice_in_dim(dec_q, head, WIDTH, 2)]
    slice x22 -> x0, local copies, waits for them, and re-layouts: 15.9 us -> none  [the longest x16 15.9 us: fold_keys(): single_values = value_block[key_half].reshape(key_width, kv_dev, HEAD_WIDTH)]
    reduce_sum x38 -> x0, other arithmetic: 15.7 us -> none  [absorb(): weight_sum = weight_sum * shrink + jnp.sum(exponent, axis=-1)]
  transfers between devices with their start and end apart: 3 -> 0, of which waited for: 2 -> 0; matrix products, arithmetic and copies ran while one was open for 6% -> 0% of each run, Pallas kernels for 0% -> 0%
where the time goes in v1:
time: 84.4 us; the launch traced here: 84.2 us
  Pallas kernels  80.1 us (95%)
  local copies, waits for them, and re-layouts  2.54 us (3%)
    pallas_call x1, Pallas kernels, local(): pl.pallas_call(kernel, out_shape=(jax.ShapeDtypeStruct((2, TOK, GROUP * W...  80.1 us

profile of v1, /device:TPU:8, one launch (start us, length us, event | category | flops | bytes accessed | tf_op | source)
XLA Modules:
  0.0 84.2 jit_solution(603475077095926558)
XLA Ops:
  0.6 0.0 copy-start
  0.6 0.0 copy-start.1
  0.7 0.9 %copy-done = bf16[40,4,1024]{2,1,0:T(4,128)(2,1)S(1)} copy-done((bf16[40,4,1024]{2,1,0:T(4,128)(2,1)S(1)}, bf16[40,4,1024]{2,1,0:T(4,128)(2,1)}, u32[]{:S(2)}) %copy-start) | copy-done | bytes 327704
  1.6 0.0 copy-start.2
  1.6 0.0 copy-start.3
  1.7 0.8 pad_maximum_fusion.dqkv
  2.5 0.0 copy-done.1
  2.5 0.0 copy-done.2
  2.5 0.0 copy-done.3
  2.5 80.1 %shard_map.77 = (bf16[2,64,1024]{2,1,0:T(8,128)(2,1)S(1)}, bf16[160,1024]{1,0:T(8,128)(2,1)S(1)}) custom-call(bf16[2,64,1024]{2,1,0:T(8,128)(2,1)S(1)} %copy-done.1, bf16[2,64,128]{2,1,0:T(8,128)(2,1)S(1)} %copy-done.2, bf16[2,64,128]{2,1,0:T(8,128)(2,1)S(1)} %copy-done.3, bf16[3,160,128]{2,1,0:T(8,128)(2,1)S(1)} %pad_maximum_fusion.dqkv), custom_call_target="tpu_custom_call" | custom-call | tf_op jit(solution)/shard_map/pallas_call | solution.py:447
  82.6 0.9 %reshape.14 = bf16[40,4,1024]{2,1,0:T(4,128)(2,1)} reshape(bf16[160,1024]{1,0:T(8,128)(2,1)S(1)} %get-tuple-element.5) | data formatting | bytes 655360 | tf_op jit(solution)/shard_map/reshape | solution.py:484
  83.5 0.7 copy.9
  (1 shorter events, 0.0 us)
Async XLA Ops:
  0.6 1.0 %copy-start = (bf16[40,4,1024]{2,1,0:T(4,128)(2,1)S(1)}, bf16[40,4,1024]{2,1,0:T(4,128)(2,1)}, u32[]{:S(2)}) copy-start(bf16[40,4,1024]{2,1,0:T(4,128)(2,1)} %param.9) | copy-start | bytes 983044
  0.6 1.8 %copy-start.1 = (bf16[2,64,1024]{2,1,0:T(8,128)(2,1)S(1)}, bf16[2,64,1024]{2,1,0:T(8,128)(2,1)}, u32[]{:S(2)}) copy-start(bf16[2,64,1024]{2,1,0:T(8,128)(2,1)} %pq.1) | copy-start | bytes 786436
  1.6 0.9 %copy-start.2 = (bf16[2,64,128]{2,1,0:T(8,128)(2,1)S(1)}, bf16[2,64,128]{2,1,0:T(8,128)(2,1)}, u32[]{:S(2)}) copy-start(bf16[2,64,128]{2,1,0:T(8,128)(2,1)} %pk.1) | copy-start | bytes 98308
  1.6 0.9 %copy-start.3 = (bf16[2,64,128]{2,1,0:T(8,128)(2,1)S(1)}, bf16[2,64,128]{2,1,0:T(8,128)(2,1)}, u32[]{:S(2)}) copy-start(bf16[2,64,128]{2,1,0:T(8,128)(2,1)} %pv.1) | copy-start | bytes 98308

commit v2 on v1

v2 whole, which is shorter than its diff:
```python
import math

import jax
import jax.numpy as jnp
from jax import lax
from jax.experimental import pallas as pl
from jax.experimental.pallas import tpu as pltpu
from jax.sharding import PartitionSpec as P

WIDTH = 128
MESH = pl.DeviceIdType.MESH
SCALE = math.log2(math.e) / math.sqrt(WIDTH)
LOW = -1e30
NT = (((1,), (1,)), ((), ()))
NX, NY, NZ = 4, 8, 4
TOK = 64
GROUP = 8
HALF = TOK * GROUP
MAIN = 2 * HALF
DEC = 160
ROWS = MAIN + DEC
KEYS = NY * TOK
BLOCK = 128
PART = KEYS // 2
F32, BF16 = jnp.float32, jnp.bfloat16


def kernel(
    pq, pk, pv, dqkv, out, dout,
    qbuf, kv, acc, top, part, stat, got, gstat, dgat,
    zs, zr, ys, yr, qs, qr, fs, fr, ds, dr,
):
    rep, y, tp = lax.axis_index("rep"), lax.axis_index("seq"), lax.axis_index("tp")
    z, x = rep // NX, rep % NX

    def at(zz, xx, yy):
        return (zz * NX + xx, yy, tp)

    along_x = [at(z, (x + j) % NX, y) for j in range(NX)]
    along_y = [at(z, x, (y + j) % NY) for j in range(NY)]
    along_z = [at((z + j) % NZ, x, y) for j in range(NZ)]
    peers = along_x[1:] + along_y[1:] + along_z[1:]

    def send(src, dst, ssem, rsem, dev):
        return pltpu.make_async_remote_copy(
            src_ref=src, dst_ref=dst, send_sem=ssem, recv_sem=rsem, device_id=dev, device_id_type=MESH
        )

    def start(copies):
        for copy in copies:
            copy.start()

    def arrive(copies):
        for copy in copies:
            copy.wait_recv()

    barrier = pltpu.get_barrier_semaphore()
    for dev in peers:
        pl.semaphore_signal(barrier, inc=1, device_id=dev, device_id_type=MESH)

    kv[z, :, 0, 0:TOK, 0:WIDTH] = pk[...]
    kv[z, :, 0, 0:TOK, WIDTH : 2 * WIDTH] = pv[...]
    for half in range(2):
        for g in range(GROUP):
            qbuf[0, half * HALF + g * TOK : half * HALF + (g + 1) * TOK, :] = pq[
                half, :, g * WIDTH : (g + 1) * WIDTH
            ]
    qbuf[0, MAIN:ROWS, :] = dqkv[0]

    pl.semaphore_wait(barrier, len(peers))

    planes = (
        z,
        jnp.where(z == 0, 1, z - 1),
        jnp.where(z < 2, 2, jnp.where(z == 2, 3, 1)),
        jnp.where(z < 2, 3, 0),
    )

    def plane_at(k):
        return jnp.where(k == 0, planes[0], jnp.where(k == 1, planes[1], jnp.where(k == 2, planes[2], planes[3])))

    def slot(p, r):
        return kv.at[p, :, r // 4, pl.ds(r % 4 * TOK, TOK), :]

    def slot_half(p, r, half):
        return kv.at[p, half, r // 4, pl.ds(r % 4 * TOK, TOK), :]

    def z_copy(j):
        own = slot(z, 0)
        return send(own, own, zs.at[j - 1], zr.at[z], along_z[j])

    def z_arrive(p):
        here = slot(p, 0)
        send(here, here, zs.at[0], zr.at[p], along_z[1]).wait_recv()

    def ring_copies(p, d):
        a, b = (0, 0) if d == 1 else (2 * d - 3, 2 * d - 2)
        if d < 4:
            pairs = (slot(p, a), slot(p, 2 * d - 1)), (slot(p, b), slot(p, 2 * d))
        else:
            pairs = (slot_half(p, a, 0), slot_half(p, 7, 0)), (slot_half(p, b, 1), slot_half(p, 7, 1))
        return [
            send(*pair, ys.at[p, 2 * d - 2 + i], yr.at[p, 2 * d - 2 + i], along_y[1 - 2 * i])
            for i, pair in enumerate(pairs)
        ]

    def steps(k):
        return [ring_copies(planes[k], d) for d in range(1, 5)]

    def z_step(k):
        if k == 0:
            for j in range(1, NZ):
                z_copy(j).start()
        else:
            z_arrive(planes[k])
        start(steps(k)[0])

    def y_step(k, d):
        arrive(steps(k)[d - 1])
        if d < len(steps(k)):
            start(steps(k)[d])

    def q_copy(j):
        return send(qbuf.at[0], qbuf.at[j], qs.at[j - 1], qr.at[j - 1], along_x[j])

    def values(half, *items):
        def columns(first):
            parts = [kv[p, half, group, :, first : first + WIDTH] for p, group in items]
            return parts[0] if len(parts) == 1 else jnp.concatenate(parts, axis=0)

        v = columns(WIDTH)
        return columns(0), jnp.concatenate([v, jnp.ones_like(v)], axis=1)

    def update(s, r0, n, keys, vals, allowed=None):
        rows = pl.ds(r0, n)
        scores = lax.dot_general(qbuf[s, rows, :], keys, NT, preferred_element_type=F32)
        if allowed is not None:
            scores = jnp.where(allowed, scores, LOW)
        top_old = top[s, rows, :]
        top_new = jnp.maximum(top_old, jnp.max(scores, axis=-1, keepdims=True) * SCALE)
        shrink = jnp.exp2(top_old - top_new)
        span = scores.shape[1]
        anchor = top_new[:, 0:1] if span % WIDTH else jnp.tile(top_new, (1, span // WIDTH))
        weights = jnp.exp2(scores * SCALE - anchor).astype(BF16)
        top[s, rows, :] = top_new
        acc[s, rows, :] = acc[s, rows, :] * jnp.concatenate([shrink, shrink], axis=1) + jnp.dot(
            weights, vals, preferred_element_type=F32
        )

    def main_rows(s, items, halves):
        k0, v0 = values(0, *items)
        for j in range(HALF // BLOCK):
            update(s, HALF + j * BLOCK, BLOCK, k0, v0)
        for item, h in zip(items, halves):
            kh, vh = values(h, item)
            for j in range(HALF // BLOCK):
                update(s, pl.multiple_of(h * HALF + j * BLOCK, BLOCK), BLOCK, kh, vh)

    def sampled(item, carry):
        for half in range(2):
            kk, vv = values(half, (plane_at(item % NZ), item // NZ))
            for s in range(4):
                update(s, MAIN, DEC, kk, vv)
        return carry

    def which(s, k, p):
        far = (x + NX - s) % NX
        return jnp.where(k == 0, jnp.where(x < far, 0, 1), jnp.where(p < z, 0, 1))

    def eye(n):
        return lax.broadcasted_iota(jnp.int32, (n, WIDTH), 0) == lax.broadcasted_iota(jnp.int32, (n, WIDTH), 1)

    def finish(s, r0, n, target, starget, row, count):
        rows = pl.ds(r0, n)
        total = acc[s, rows, WIDTH : 2 * WIDTH]
        target[rows, :] = (acc[s, rows, 0:WIDTH] / jnp.maximum(total, 1e-30)).astype(BF16)
        mask = eye(n)
        starget[row : row + 1, :] = jnp.sum(jnp.where(mask, top[s, rows, :], 0.0), axis=0, keepdims=True)
        starget[row + count : row + count + 1, :] = jnp.sum(jnp.where(mask, total, 0.0), axis=0, keepdims=True)

    def merge(s, r0, n, source, ssource, row, count):
        rows = pl.ds(r0, n)
        mask = eye(n)

        def column(r):
            return jnp.sum(jnp.where(mask, ssource[r : r + 1, :], 0.0), axis=1, keepdims=True)

        top_in, sum_in = column(row), column(row + count)
        top_old = top[s, rows, :]
        top_new = jnp.maximum(top_old, top_in)
        shrink = jnp.exp2(top_old - top_new)
        gain = jnp.exp2(top_in - top_new) * sum_in
        top[s, rows, :] = top_new
        acc[s, rows, 0:WIDTH] = acc[s, rows, 0:WIDTH] * shrink + source[rows, :].astype(F32) * gain
        acc[s, rows, WIDTH : 2 * WIDTH] = acc[s, rows, WIDTH : 2 * WIDTH] * shrink + gain

    def section(c):
        if c < 2:
            return [(c * HALF + j * BLOCK, BLOCK, c, j) for j in range(4)], 4, pl.ds(c * HALF, HALF), pl.ds(c, 1)
        half = DEC // 2
        return [(MAIN + j * half, half, 2 + j, 0) for j in range(2)], 1, pl.ds(MAIN, DEC), pl.ds(2, 2)

    def final_copies(s, c):
        _, _, rows, sheets = section(c)
        i, owner = 3 * (s - 1) + c, at(z, (x + NX - s) % NX, y)
        return [
            send(part.at[s, rows, :], got.at[s - 1, rows, :], fs.at[i], fr.at[i], owner),
            send(stat.at[s, sheets], gstat.at[s - 1, sheets], fs.at[9 + i], fr.at[9 + i], owner),
        ]

    def give(s, c):
        blocks, count, _, _ = section(c)
        for r0, n, sheet, j in blocks:
            finish(s, r0, n, part.at[s], stat.at[s, sheet], j, count)
        start(final_copies(s, c))

    def take(s, c):
        arrive(final_copies(s, c))
        blocks, count, _, _ = section(c)
        for r0, n, sheet, j in blocks:
            merge(0, r0, n, got.at[s - 1], gstat.at[s - 1, sheet], j, count)

    def give_sampled(s, carry):
        give(s, 2)
        return carry

    def take_sampled(s, carry):
        take(s, 2)
        return carry

    def d_copy(j):
        return send(dgat.at[0], dgat.at[j], ds.at[j - 1], dr.at[j - 1], along_y[j])

    def place(j):
        column = pl.multiple_of(((y + NY - j) % NY) * WIDTH, WIDTH)
        dout[:, pl.ds(column, WIDTH)] = dgat[j]

    z_step(0)
    q_copy(1).start()
    q_copy(3).start()

    def clear(s, carry):
        acc[s] = jnp.zeros((ROWS, 2 * WIDTH), F32)
        top[s] = jnp.full((ROWS, WIDTH), LOW, F32)
        return carry

    lax.fori_loop(0, 4, clear, 0)

    step_row = lax.broadcasted_iota(jnp.int32, (DEC, DEC), 0)
    step_col = lax.broadcasted_iota(jnp.int32, (DEC, DEC), 1)
    own_v = dqkv[2]
    update(
        0, MAIN, DEC, dqkv[1], jnp.concatenate([own_v, jnp.ones_like(own_v)], axis=1),
        (step_row // 4 == step_col // 4) & (step_col <= step_row),
    )

    def own_plane(group):
        shape = (BLOCK, PART)
        key = group * PART + lax.broadcasted_iota(jnp.int32, shape, 1)
        key_slot = key // TOK
        key_delta = jnp.where(key_slot % 2 == 1, NY - (key_slot + 1) // 2, key_slot // 2)
        key_index = ((y + key_delta) % NY) * TOK + key % TOK
        query_index = y * TOK + lax.broadcasted_iota(jnp.int32, shape, 0) % TOK
        k0, v0 = values(0, (planes[0], group))
        k1, v1 = values(1, (planes[0], group))
        for j in range(HALF // BLOCK):
            update(0, HALF + j * BLOCK, BLOCK, k0, v0)
            update(0, j * BLOCK, BLOCK, k0, v0, key_index <= query_index)
        for j in range(HALF // BLOCK):
            update(0, HALF + j * BLOCK, BLOCK, k1, v1, key_index >= query_index)

    y_step(0, 1)
    q_copy(2).start()
    for k in range(1, NZ):
        z_step(k)
    for k in range(1, NZ):
        y_step(k, 1)
    y_step(0, 2)

    unit_rows = (0, 1, 3, 2, 0, 1, 3, 2, 2, 1, 2, 1, 3, 3, 0, 0)
    unit_one = (0, 0, 0, 0, 2, 4, 4, 4, 1, 1, 5, 5, 1, 5, 6, 5)
    unit_two = (0, 2, 2, 2, 4, 6, 6, 6, 3, 3, 7, 7, 3, 7, 3, 7)

    def lookup(table, t):
        value = jnp.int32(table[0])
        for i in range(1, len(table)):
            value = jnp.where(t == i, table[i], value)
        return value

    def sampled_out():
        lax.fori_loop(1, NX, take_sampled, 0)
        rows = pl.ds(MAIN, DEC)
        dgat[0] = (acc[0, rows, 0:WIDTH] / acc[0, rows, WIDTH : 2 * WIDTH]).astype(BF16)
        start([d_copy(j) for j in range(1, NY)])
        place(0)

    after = {
        0: [lambda: y_step(1, 2)],
        1: [lambda: y_step(2, 2)],
        2: [lambda: y_step(3, 2)],
        3: [lambda: y_step(0, 3)],
        4: [lambda: y_step(1, 3)],
        5: [lambda: y_step(2, 3)],
        6: [lambda: y_step(3, 3), lambda: y_step(0, 4)],
        7: [lambda: y_step(1, 4)],
        8: [lambda: y_step(2, 4)],
        9: [lambda: y_step(3, 4)],
        12: [sampled_out],
    }
    met = (0, 0, 0, 1, 2, 3, 4, 4, 5, 8, 8, 8, 8, 8, 8, 8)

    before = {
        1: [lambda: q_copy(1).wait_recv()],
        2: [lambda: q_copy(3).wait_recv()],
        3: [lambda: q_copy(2).wait_recv()],
    }

    def hook(table, t):
        for i, work in table.items():

            @pl.when(t == i)
            def _(work=work):
                for step in work:
                    step()

    def unit(t, carry):
        hook(before, t)
        s = lookup(unit_rows, t)

        @pl.when((t == 0) | (t == 8))
        def _():
            own_plane(jnp.where(t == 0, 0, 1))

        @pl.when(t > 0)
        def _():
            items, halves = [], []
            for table in (unit_one, unit_two):
                item = lookup(table, t)
                k, group = item // 2, item % 2
                p = plane_at(k)
                items.append((p, group))
                halves.append(which(s, k, p))
            main_rows(s, items, halves)

        hook(after, t)
        lax.fori_loop(lookup(met, t - 1), lookup(met, t), sampled, 0)

        @pl.when(t == 9)
        def _():
            lax.fori_loop(1, NX, give_sampled, 0)

        @pl.when((t == 10) | (t == 11) | (t == 13))
        def _():
            give(s, 0)
            give(s, 1)

        return carry

    lax.fori_loop(0, 16, unit, 0)

    def take_main(i, carry):
        s = lookup((2, 1, 3), i)
        take(s, 0)
        take(s, 1)
        return carry

    lax.fori_loop(0, 3, take_main, 0)
    for c in range(2):
        for g in range(GROUP):
            rows = pl.ds(c * HALF + g * TOK, TOK)
            out[c, :, g * WIDTH : (g + 1) * WIDTH] = (
                acc[0, rows, 0:WIDTH] / acc[0, rows, WIDTH : 2 * WIDTH]
            ).astype(BF16)
    for j in range(1, NY):
        d_copy(j).wait_recv()
        place(j)

    gone = [z_copy(j) for j in range(1, NZ)] + [q_copy(j) for j in range(1, NX)] + [d_copy(j) for j in range(1, NY)]
    for k in range(NZ):
        for copies in steps(k):
            gone += copies
    for s in range(1, NX):
        for c in range(3):
            gone += final_copies(s, c)
    for copy in gone:
        copy.wait_send()


def local(prompt_q, prompt_k, prompt_v, dec_q, dec_k, dec_v):
    head = lax.axis_index("seq") * WIDTH
    mine = lax.dynamic_slice_in_dim(dec_q, head, WIDTH, 2)
    dqkv = jnp.stack([mine, dec_k, dec_v]).reshape(3, DEC, WIDTH)
    vmem = pl.BlockSpec(memory_space=pltpu.VMEM)
    dma = pltpu.SemaphoreType.DMA
    prefill_out, decode_out = pl.pallas_call(
        kernel,
        out_shape=(
            jax.ShapeDtypeStruct((2, TOK, GROUP * WIDTH), BF16),
            jax.ShapeDtypeStruct((DEC, GROUP * WIDTH), BF16),
        ),
        in_specs=[vmem] * 4,
        out_specs=(vmem, vmem),
        scratch_shapes=[
            pltpu.VMEM((4, ROWS, WIDTH), BF16),
            pltpu.VMEM((NZ, 2, 2, PART, 2 * WIDTH), BF16),
            pltpu.VMEM((4, ROWS, 2 * WIDTH), F32),
            pltpu.VMEM((4, ROWS, WIDTH), F32),
            pltpu.VMEM((4, ROWS, WIDTH), BF16),
            pltpu.VMEM((4, 4, 8, WIDTH), F32),
            pltpu.VMEM((3, ROWS, WIDTH), BF16),
            pltpu.VMEM((3, 4, 8, WIDTH), F32),
            pltpu.VMEM((NY, DEC, WIDTH), BF16),
            dma((NZ - 1,)),
            dma((NZ,)),
            dma((NZ, 8)),
            dma((NZ, 8)),
            dma((NX - 1,)),
            dma((NX - 1,)),
            dma((18,)),
            dma((18,)),
            dma((NY - 1,)),
            dma((NY - 1,)),
        ],
        compiler_params=pltpu.CompilerParams(
            collective_id=0, has_side_effects=True, vmem_limit_bytes=48 << 20
        ),
    )(prompt_q, prompt_k, prompt_v, dqkv)
    return prefill_out, decode_out.reshape(dec_q.shape)


def solution(mesh):
    placed = (
        P(None, ("rep", "seq"), "tp"),
        P(None, ("rep", "seq"), "tp"),
        P(None, ("rep", "seq"), "tp"),
        P("rep", None, "tp"),
        P("rep", None, "tp"),
        P("rep", None, "tp"),
    )
    return jax.shard_map(
        local,
        mesh=mesh,
        in_specs=placed,
        out_specs=(P(None, ("rep", "seq"), "tp"), P("rep", None, "tp")),
        check_vma=False,
    )
```

time: 84.4 us -> 63.5 us (0.75)
  the two profiles are of different devices: /device:TPU:8 before, /device:TPU:24 now
where the time goes in v2:
time: 63.5 us; the launch traced here: 63.3 us
  Pallas kernels  59.2 us (93%)
  local copies, waits for them, and re-layouts  2.54 us (4%)
  other arithmetic  0.82 us (1%)
  between operations  0.7 us (1%)
    pallas_call x1, Pallas kernels, local(): pl.pallas_call(kernel, out_shape=(jax.ShapeDtypeStruct((2, TOK, GROUP * W...  59.2 us
    unnamed x9, local copies, waits for them, and re-layouts  1.68 us

profile of v2, /device:TPU:24, one launch (start us, length us, event | category | flops | bytes accessed | tf_op | source)
XLA Modules:
  0.0 63.3 jit_solution(761776364199783481)
XLA Ops:
  0.6 0.0 copy-start
  0.6 0.0 copy-start.1
  0.7 0.9 %copy-done = bf16[40,4,1024]{2,1,0:T(4,128)(2,1)S(1)} copy-done((bf16[40,4,1024]{2,1,0:T(4,128)(2,1)S(1)}, bf16[40,4,1024]{2,1,0:T(4,128)(2,1)}, u32[]{:S(2)}) %copy-start) | copy-done | bytes 327704
  1.6 0.0 copy-start.2
  1.6 0.0 copy-start.3
  1.7 0.8 %pad_maximum_fusion.dqkv = bf16[3,160,128]{2,1,0:T(8,128)(2,1)S(1)} fusion(bf16[1,160,128]{2,1,0:T(8,128)(2,1)} %bitcast.4, bf16[1,160,128]{2,1,0:T(8,128)(2,1)} %bitcast.5, bf16[1,160,128]{2,1,0:T(8,128)(2,1)S(1)} %bitcast.3), kind=kLoop, calls=%fused_computation | loop fusion | flops 122880 | bytes 245760 | tf_op jit(solution)/shard_map/stack | solution.py:392
  2.5 0.0 copy-done.1
  2.5 0.0 copy-done.2
  2.5 0.0 copy-done.3
  2.5 59.2 %shard_map.77 = (bf16[2,64,1024]{2,1,0:T(8,128)(2,1)S(1)}, bf16[160,1024]{1,0:T(8,128)(2,1)S(1)}) custom-call(bf16[2,64,1024]{2,1,0:T(8,128)(2,1)S(1)} %copy-done.1, bf16[2,64,128]{2,1,0:T(8,128)(2,1)S(1)} %copy-done.2, bf16[2,64,128]{2,1,0:T(8,128)(2,1)S(1)} %copy-done.3, bf16[3,160,128]{2,1,0:T(8,128)(2,1)S(1)} %pad_maximum_fusion.dqkv), custom_call_target="tpu_custom_call" | custom-call | tf_op jit(solution)/shard_map/pallas_call | solution.py:395
  61.7 0.9 %reshape.14 = bf16[40,4,1024]{2,1,0:T(4,128)(2,1)} reshape(bf16[160,1024]{1,0:T(8,128)(2,1)S(1)} %get-tuple-element.5) | data formatting | bytes 655360 | tf_op jit(solution)/shard_map/reshape | solution.py:428
  62.6 0.7 %copy.9 = bf16[2,64,1024]{2,1,0:T(8,128)(2,1)} copy(bf16[2,64,1024]{2,1,0:T(8,128)(2,1)S(1)} %get-tuple-element.8) | data formatting | bytes 524288
  (1 shorter events, 0.0 us)
Async XLA Ops:
  0.6 1.0 %copy-start = (bf16[40,4,1024]{2,1,0:T(4,128)(2,1)S(1)}, bf16[40,4,1024]{2,1,0:T(4,128)(2,1)}, u32[]{:S(2)}) copy-start(bf16[40,4,1024]{2,1,0:T(4,128)(2,1)} %param.9) | copy-start | bytes 983044
  0.6 1.8 %copy-start.1 = (bf16[2,64,1024]{2,1,0:T(8,128)(2,1)S(1)}, bf16[2,64,1024]{2,1,0:T(8,128)(2,1)}, u32[]{:S(2)}) copy-start(bf16[2,64,1024]{2,1,0:T(8,128)(2,1)} %pq.1) | copy-start | bytes 786436
  1.6 0.9 %copy-start.2 = (bf16[2,64,128]{2,1,0:T(8,128)(2,1)S(1)}, bf16[2,64,128]{2,1,0:T(8,128)(2,1)}, u32[]{:S(2)}) copy-start(bf16[2,64,128]{2,1,0:T(8,128)(2,1)} %pk.1) | copy-start | bytes 98308
  1.6 0.9 %copy-start.3 = (bf16[2,64,128]{2,1,0:T(8,128)(2,1)S(1)}, bf16[2,64,128]{2,1,0:T(8,128)(2,1)}, u32[]{:S(2)}) copy-start(bf16[2,64,128]{2,1,0:T(8,128)(2,1)} %pv.1) | copy-start | bytes 98308

commit v3 on v2

--- a/solution.py
+++ b/solution.py
@@ -85,13 +85,14 @@
     def slot_half(p, r, half):
         return kv.at[p, half, r // 4, pl.ds(r % 4 * TOK, TOK), :]
 
-    def z_copy(j):
-        own = slot(z, 0)
-        return send(own, own, zs.at[j - 1], zr.at[z], along_z[j])
-
-    def z_arrive(p):
-        here = slot(p, 0)
-        send(here, here, zs.at[0], zr.at[p], along_z[1]).wait_recv()
+    def z_copy(i, r=0):
+        own = slot(z, r)
+        j = (i - 1) + (NZ - 1) * (r > 0)
+        return send(own, own, zs.at[j], zr.at[z, int(r > 0)], at(planes[i], x, y))
+
+    def z_arrive(p, r=0):
+        here = slot(p, r)
+        send(here, here, zs.at[0], zr.at[p, int(r > 0)], along_z[1]).wait_recv()
 
     def ring_copies(p, d):
         a, b = (0, 0) if d == 1 else (2 * d - 3, 2 * d - 2)
@@ -105,12 +106,12 @@
         ]
 
     def steps(k):
-        return [ring_copies(planes[k], d) for d in range(1, 5)]
+        return [ring_copies(planes[k], d) for d in range(1, 5 if k == 0 else 4)]
 
     def z_step(k):
         if k == 0:
-            for j in range(1, NZ):
-                z_copy(j).start()
+            for i in range(1, NZ):
+                z_copy(i).start()
         else:
             z_arrive(planes[k])
         start(steps(k)[0])
@@ -119,6 +120,12 @@
         arrive(steps(k)[d - 1])
         if d < len(steps(k)):
             start(steps(k)[d])
+        elif k == 0:
+            for i in range(1, NZ):
+                z_copy(i, 7).start()
+
+    def far_step(k):
+        z_arrive(planes[k], 7)
 
     def q_copy(j):
         return send(qbuf.at[0], qbuf.at[j], qs.at[j - 1], qr.at[j - 1], along_x[j])
@@ -158,7 +165,8 @@
 
     def sampled(item, carry):
         for half in range(2):
-            kk, vv = values(half, (plane_at(item % NZ), item // NZ))
+            first = item % 2 * 2
+            kk, vv = values(half, (plane_at(first), item // 2), (plane_at(first + 1), item // 2))
             for s in range(4):
                 update(s, MAIN, DEC, kk, vv)
         return carry
@@ -238,6 +246,9 @@
     z_step(0)
     q_copy(1).start()
     q_copy(3).start()
+
+    y_step(0, 1)
+    z_step(1)
 
     def clear(s, carry):
         acc[s] = jnp.zeros((ROWS, 2 * WIDTH), F32)
@@ -269,17 +280,15 @@
         for j in range(HALF // BLOCK):
             update(0, HALF + j * BLOCK, BLOCK, k1, v1, key_index >= query_index)
 
-    y_step(0, 1)
+    y_step(0, 2)
     q_copy(2).start()
-    for k in range(1, NZ):
-        z_step(k)
-    for k in range(1, NZ):
-        y_step(k, 1)
-    y_step(0, 2)
-
-    unit_rows = (0, 1, 3, 2, 0, 1, 3, 2, 2, 1, 2, 1, 3, 3, 0, 0)
-    unit_one = (0, 0, 0, 0, 2, 4, 4, 4, 1, 1, 5, 5, 1, 5, 6, 5)
-    unit_two = (0, 2, 2, 2, 4, 6, 6, 6, 3, 3, 7, 7, 3, 7, 3, 7)
+    z_step(2)
+    z_step(3)
+    y_step(1, 1)
+
+    unit_rows = (0, 1, 3, 0, 1, 3, 2, 2, 2, 2, 1, 1, 3, 3, 0, 0)
+    unit_one = (0, 0, 0, 2, 4, 4, 0, 4, 1, 5, 1, 5, 1, 5, 6, 5)
+    unit_two = (0, 2, 2, 4, 6, 6, 2, 6, 3, 7, 3, 7, 3, 7, 3, 7)
 
     def lookup(table, t):
         value = jnp.int32(table[0])
@@ -295,24 +304,22 @@
         place(0)
 
     after = {
-        0: [lambda: y_step(1, 2)],
-        1: [lambda: y_step(2, 2)],
+        0: [lambda: y_step(0, 3), lambda: y_step(2, 1), lambda: y_step(3, 1), lambda: y_step(1, 2)],
+        1: [lambda: y_step(0, 4), lambda: y_step(2, 2)],
         2: [lambda: y_step(3, 2)],
-        3: [lambda: y_step(0, 3)],
-        4: [lambda: y_step(1, 3)],
-        5: [lambda: y_step(2, 3)],
-        6: [lambda: y_step(3, 3), lambda: y_step(0, 4)],
-        7: [lambda: y_step(1, 4)],
-        8: [lambda: y_step(2, 4)],
-        9: [lambda: y_step(3, 4)],
-        12: [sampled_out],
+        3: [lambda: y_step(1, 3)],
+        4: [lambda: y_step(2, 3)],
+        5: [lambda: y_step(3, 3)],
+        7: [lambda: far_step(1)],
+        8: [lambda: far_step(2), lambda: far_step(3)],
+        11: [sampled_out],
     }
-    met = (0, 0, 0, 1, 2, 3, 4, 4, 5, 8, 8, 8, 8, 8, 8, 8)
+    met = (0, 0, 0, 0, 0, 0, 1, 3, 4, 4, 4, 4, 4, 4, 4, 4)
 
     before = {
         1: [lambda: q_copy(1).wait_recv()],
         2: [lambda: q_copy(3).wait_recv()],
-        3: [lambda: q_copy(2).wait_recv()],
+        6: [lambda: q_copy(2).wait_recv()],
     }
 
     def hook(table, t):
@@ -345,11 +352,11 @@
         hook(after, t)
         lax.fori_loop(lookup(met, t - 1), lookup(met, t), sampled, 0)
 
-        @pl.when(t == 9)
+        @pl.when(t == 8)
         def _():
             lax.fori_loop(1, NX, give_sampled, 0)
 
-        @pl.when((t == 10) | (t == 11) | (t == 13))
+        @pl.when((t == 9) | (t == 11) | (t == 13))
         def _():
             give(s, 0)
             give(s, 1)
@@ -375,7 +382,8 @@
         d_copy(j).wait_recv()
         place(j)
 
-    gone = [z_copy(j) for j in range(1, NZ)] + [q_copy(j) for j in range(1, NX)] + [d_copy(j) for j in range(1, NY)]
+    gone = [z_copy(i, r) for i in range(1, NZ) for r in (0, 7)]
+    gone += [q_copy(j) for j in range(1, NX)] + [d_copy(j) for j in range(1, NY)]
     for k in range(NZ):
         for copies in steps(k):
             gone += copies
@@ -410,8 +418,8 @@
             pltpu.VMEM((3, ROWS, WIDTH), BF16),
             pltpu.VMEM((3, 4, 8, WIDTH), F32),
             pltpu.VMEM((NY, DEC, WIDTH), BF16),
-            dma((NZ - 1,)),
-            dma((NZ,)),
+            dma((2 * NZ - 2,)),
+            dma((NZ, 2)),
             dma((NZ, 8)),
             dma((NZ, 8)),
             dma((NX - 1,)),

time: 63.5 us -> 62.7 us (0.987)
  the two profiles are of different devices: /device:TPU:24 before, /device:TPU:16 now
where the time goes in v3:
time: 62.7 us; the launch traced here: 62.5 us
  Pallas kernels  58.4 us (93%)
  local copies, waits for them, and re-layouts  2.54 us (4%)
  other arithmetic  0.82 us (1%)
  between operations  0.7 us (1%)
    pallas_call x1, Pallas kernels, local(): pl.pallas_call(kernel, out_shape=(jax.ShapeDtypeStruct((2, TOK, GROUP * W...  58.4 us
    unnamed x9, local copies, waits for them, and re-layouts  1.68 us

profile of v3, /device:TPU:16, one launch (start us, length us, event | category | flops | bytes accessed | tf_op | source)
XLA Modules:
  0.0 62.5 jit_solution(15871416195850239062)
XLA Ops:
  0.6 0.0 copy-start
  0.6 0.0 copy-start.1
  0.7 0.9 %copy-done = bf16[40,4,1024]{2,1,0:T(4,128)(2,1)S(1)} copy-done((bf16[40,4,1024]{2,1,0:T(4,128)(2,1)S(1)}, bf16[40,4,1024]{2,1,0:T(4,128)(2,1)}, u32[]{:S(2)}) %copy-start) | copy-done | bytes 327704
  1.6 0.0 copy-start.2
  1.6 0.0 copy-start.3
  1.7 0.8 %pad_maximum_fusion.dqkv = bf16[3,160,128]{2,1,0:T(8,128)(2,1)S(1)} fusion(bf16[1,160,128]{2,1,0:T(8,128)(2,1)} %bitcast.4, bf16[1,160,128]{2,1,0:T(8,128)(2,1)} %bitcast.5, bf16[1,160,128]{2,1,0:T(8,128)(2,1)S(1)} %bitcast.3), kind=kLoop, calls=%fused_computation | loop fusion | flops 122880 | bytes 245760 | tf_op jit(solution)/shard_map/stack | solution.py:400
  2.5 0.0 copy-done.1
  2.5 0.0 copy-done.2
  2.5 0.0 copy-done.3
  2.5 58.4 %shard_map.77 = (bf16[2,64,1024]{2,1,0:T(8,128)(2,1)S(1)}, bf16[160,1024]{1,0:T(8,128)(2,1)S(1)}) custom-call(bf16[2,64,1024]{2,1,0:T(8,128)(2,1)S(1)} %copy-done.1, bf16[2,64,128]{2,1,0:T(8,128)(2,1)S(1)} %copy-done.2, bf16[2,64,128]{2,1,0:T(8,128)(2,1)S(1)} %copy-done.3, bf16[3,160,128]{2,1,0:T(8,128)(2,1)S(1)} %pad_maximum_fusion.dqkv), custom_call_target="tpu_custom_call" | custom-call | tf_op jit(solution)/shard_map/pallas_call | solution.py:403
  60.9 0.9 %reshape.14 = bf16[40,4,1024]{2,1,0:T(4,128)(2,1)} reshape(bf16[160,1024]{1,0:T(8,128)(2,1)S(1)} %get-tuple-element.5) | data formatting | bytes 655360 | tf_op jit(solution)/shard_map/reshape | solution.py:436
  61.8 0.7 %copy.9 = bf16[2,64,1024]{2,1,0:T(8,128)(2,1)} copy(bf16[2,64,1024]{2,1,0:T(8,128)(2,1)S(1)} %get-tuple-element.8) | data formatting | bytes 524288
  (1 shorter events, 0.0 us)
Async XLA Ops:
  0.6 1.0 %copy-start = (bf16[40,4,1024]{2,1,0:T(4,128)(2,1)S(1)}, bf16[40,4,1024]{2,1,0:T(4,128)(2,1)}, u32[]{:S(2)}) copy-start(bf16[40,4,1024]{2,1,0:T(4,128)(2,1)} %param.9) | copy-start | bytes 983044
  0.6 1.8 %copy-start.1 = (bf16[2,64,1024]{2,1,0:T(8,128)(2,1)S(1)}, bf16[2,64,1024]{2,1,0:T(8,128)(2,1)}, u32[]{:S(2)}) copy-start(bf16[2,64,1024]{2,1,0:T(8,128)(2,1)} %pq.1) | copy-start | bytes 786436
  1.6 0.9 %copy-start.2 = (bf16[2,64,128]{2,1,0:T(8,128)(2,1)S(1)}, bf16[2,64,128]{2,1,0:T(8,128)(2,1)}, u32[]{:S(2)}) copy-start(bf16[2,64,128]{2,1,0:T(8,128)(2,1)} %pk.1) | copy-start | bytes 98308
  1.6 0.9 %copy-start.3 = (bf16[2,64,128]{2,1,0:T(8,128)(2,1)S(1)}, bf16[2,64,128]{2,1,0:T(8,128)(2,1)}, u32[]{:S(2)}) copy-start(bf16[2,64,128]{2,1,0:T(8,128)(2,1)} %pv.1) | copy-start | bytes 98308

commit v4 on v3

--- a/solution.py
+++ b/solution.py
@@ -334,7 +334,7 @@
         hook(before, t)
         s = lookup(unit_rows, t)
 
-        @pl.when((t == 0) | (t == 8))
+        @pl.when((t == 0) | (t == 14))
         def _():
             own_plane(jnp.where(t == 0, 0, 1))
 

time: 62.7 us -> 61.8 us (0.986)
  Pallas kernels: 58.4 us -> 57.5 us
    pallas_call x1, Pallas kernels: 58.4 us -> 57.5 us  [local(): pl.pallas_call(kernel, out_shape=(jax.ShapeDtypeStruct((2, TOK, GROUP * W...]
where the time goes in v4:
time: 61.8 us; the launch traced here: 61.6 us
  Pallas kernels  57.5 us (93%)
  local copies, waits for them, and re-layouts  2.54 us (4%)
  other arithmetic  0.82 us (1%)
  between operations  0.7 us (1%)
    pallas_call x1, Pallas kernels, local(): pl.pallas_call(kernel, out_shape=(jax.ShapeDtypeStruct((2, TOK, GROUP * W...  57.5 us
    unnamed x9, local copies, waits for them, and re-layouts  1.68 us

profile of v4, /device:TPU:16, one launch (start us, length us, event | category | flops | bytes accessed | tf_op | source)
XLA Modules:
  0.0 61.6 jit_solution(9389108540664419305)
XLA Ops:
  0.6 0.0 copy-start
  0.6 0.0 copy-start.1
  0.7 0.9 %copy-done = bf16[40,4,1024]{2,1,0:T(4,128)(2,1)S(1)} copy-done((bf16[40,4,1024]{2,1,0:T(4,128)(2,1)S(1)}, bf16[40,4,1024]{2,1,0:T(4,128)(2,1)}, u32[]{:S(2)}) %copy-start) | copy-done | bytes 327704
  1.6 0.0 copy-start.2
  1.6 0.0 copy-start.3
  1.7 0.8 %pad_maximum_fusion.dqkv = bf16[3,160,128]{2,1,0:T(8,128)(2,1)S(1)} fusion(bf16[1,160,128]{2,1,0:T(8,128)(2,1)} %bitcast.4, bf16[1,160,128]{2,1,0:T(8,128)(2,1)} %bitcast.5, bf16[1,160,128]{2,1,0:T(8,128)(2,1)S(1)} %bitcast.3), kind=kLoop, calls=%fused_computation | loop fusion | flops 122880 | bytes 245760 | tf_op jit(solution)/shard_map/stack | solution.py:400
  2.5 0.0 copy-done.1
  2.5 0.0 copy-done.2
  2.5 0.0 copy-done.3
  2.5 57.5 %shard_map.77 = (bf16[2,64,1024]{2,1,0:T(8,128)(2,1)S(1)}, bf16[160,1024]{1,0:T(8,128)(2,1)S(1)}) custom-call(bf16[2,64,1024]{2,1,0:T(8,128)(2,1)S(1)} %copy-done.1, bf16[2,64,128]{2,1,0:T(8,128)(2,1)S(1)} %copy-done.2, bf16[2,64,128]{2,1,0:T(8,128)(2,1)S(1)} %copy-done.3, bf16[3,160,128]{2,1,0:T(8,128)(2,1)S(1)} %pad_maximum_fusion.dqkv), custom_call_target="tpu_custom_call" | custom-call | tf_op jit(solution)/shard_map/pallas_call | solution.py:403
  60.0 0.9 %reshape.14 = bf16[40,4,1024]{2,1,0:T(4,128)(2,1)} reshape(bf16[160,1024]{1,0:T(8,128)(2,1)S(1)} %get-tuple-element.5) | data formatting | bytes 655360 | tf_op jit(solution)/shard_map/reshape | solution.py:436
  60.9 0.7 %copy.9 = bf16[2,64,1024]{2,1,0:T(8,128)(2,1)} copy(bf16[2,64,1024]{2,1,0:T(8,128)(2,1)S(1)} %get-tuple-element.8) | data formatting | bytes 524288
  (1 shorter events, 0.0 us)
Async XLA Ops:
  0.6 1.0 %copy-start = (bf16[40,4,1024]{2,1,0:T(4,128)(2,1)S(1)}, bf16[40,4,1024]{2,1,0:T(4,128)(2,1)}, u32[]{:S(2)}) copy-start(bf16[40,4,1024]{2,1,0:T(4,128)(2,1)} %param.9) | copy-start | bytes 983044
  0.6 1.8 %copy-start.1 = (bf16[2,64,1024]{2,1,0:T(8,128)(2,1)S(1)}, bf16[2,64,1024]{2,1,0:T(8,128)(2,1)}, u32[]{:S(2)}) copy-start(bf16[2,64,1024]{2,1,0:T(8,128)(2,1)} %pq.1) | copy-start | bytes 786436
  1.6 0.9 %copy-start.2 = (bf16[2,64,128]{2,1,0:T(8,128)(2,1)S(1)}, bf16[2,64,128]{2,1,0:T(8,128)(2,1)}, u32[]{:S(2)}) copy-start(bf16[2,64,128]{2,1,0:T(8,128)(2,1)} %pk.1) | copy-start | bytes 98308
  1.6 0.9 %copy-start.3 = (bf16[2,64,128]{2,1,0:T(8,128)(2,1)S(1)}, bf16[2,64,128]{2,1,0:T(8,128)(2,1)}, u32[]{:S(2)}) copy-start(bf16[2,64,128]{2,1,0:T(8,128)(2,1)} %pv.1) | copy-start | bytes 98308
